TPU v7x, 256 devices: a whole 4x4x8 slice. The times are simulated.
256 devices in a mesh: view: 8 (over y, x_hi), seq: 32 (over x_lo, z, core).
Axes of the slice: x: 4 (x_hi: 2, x_lo: 2; x = x_hi * 2 + x_lo), y: 4, z: 8, core: 2. Of those that a mesh axis runs over, the one named last changes fastest.
Arguments:
- queries: bfloat16 [8, 4096, 1536], P('view', 'seq'), may hold values from -10 to 10
- keys: bfloat16 [8, 4096, 1536], P('view', 'seq'), may hold values from -10 to 10
- values: bfloat16 [8, 4096, 1536], P('view', 'seq'), may hold values from -6 to 6
- hidden_in: bfloat16 [8, 4096, 1536], P('view', 'seq'), may hold values from -6 to 6
- gate: float32 [8, 1536], P('view'), may hold values from 0.5 to 1.5
- w_out: bfloat16 [1536, 1536], replicated, may hold values from -0.15625 to 0.15625
Outputs:
- block_out: bfloat16 [8, 4096, 1536], P('view', 'seq')
All inputs are finite; a program needn't handle non-finite values.
Results may differ from a plain program's by a relative error of at most 0.0013.
The roundings to bfloat16 on the way count: a program that leaves them out, or rounds other values in their place, can miss the bound.
Values may be sent and summed in bfloat16 or wider, within the bound.
No kernel may reach another device: no remote copies, remote signals or barrier semaphores. Data moves between devices by JAX's collectives and lax.ppermute only.
A program may use at most 128 MiB of HBM per device.

v0:
```python
import jax
import jax.numpy as jnp
from jax import lax
from jax.sharding import PartitionSpec as P

HEAD_DIM = 64


def as_sent(array):

    def short(part):
        return part.astype(jnp.bfloat16) if part.dtype == jnp.float32 else part

    return jax.tree.map(short, array)


def attend(query, keyset, valueset):
    scores = jnp.dot(query, keyset.T, preferred_element_type=jnp.float32) * HEAD_DIM ** (-0.5)
    scores = scores - jnp.max(scores, axis=-1, keepdims=True)
    weights = jnp.exp(scores)
    weights = weights / jnp.sum(weights, axis=-1, keepdims=True)
    return jnp.dot(weights.astype(jnp.bfloat16), valueset, preferred_element_type=jnp.float32)


def pool_rows(rows):
    count = rows.shape[0]
    grouped = rows.reshape(count // 4, 4, rows.shape[1]).astype(jnp.float32)
    return jnp.mean(grouped, axis=1).astype(jnp.bfloat16)


def query_items(rows, ratio):
    count, width_all = rows.shape
    width = width_all // 8
    shaped = rows.reshape(ratio, count // ratio, 8, width).transpose(0, 2, 1, 3)
    return shaped.reshape(8 * ratio, count // ratio, width)


def copied_items(rows, ratio):
    count, width_all = rows.shape
    width = width_all // 8
    grouped = rows.reshape(count, 8, width).transpose(1, 0, 2)
    return jnp.broadcast_to(grouped[None], (ratio, 8, count, width)).reshape(
        8 * ratio, count, width
    )


def body(queries, keys, values, hidden_in, gate, w_out):
    groups = lax.axis_size("seq")
    ratio = groups // 8
    local_q = queries[0]
    local_k = keys[0]
    local_v = values[0]
    tokens, dim = local_q.shape
    width = dim // 8
    pooled_k, pooled_v = (
        lax.all_gather(pool_rows(local_k)[None], "view", axis=0, tiled=True),
        lax.all_gather(pool_rows(local_v)[None], "view", axis=0, tiled=True),
    )
    pooled_k = pooled_k.reshape(-1, dim)
    pooled_v = pooled_v.reshape(-1, dim)
    moved = (
        lax.all_to_all(query_items(local_q, ratio), "seq", split_axis=0, concat_axis=1, tiled=True),
        lax.all_to_all(
            copied_items(local_k, ratio), "seq", split_axis=0, concat_axis=1, tiled=True
        ),
        lax.all_to_all(
            copied_items(local_v, ratio), "seq", split_axis=0, concat_axis=1, tiled=True
        ),
        lax.all_to_all(
            copied_items(pooled_k, ratio), "seq", split_axis=0, concat_axis=1, tiled=True
        ),
        lax.all_to_all(
            copied_items(pooled_v, ratio), "seq", split_axis=0, concat_axis=1, tiled=True
        ),
    )
    head_q, head_k, head_v, cross_k, cross_v = [member[0] for member in moved]
    count = head_q.shape[0]
    block = min(512, count)

    def one_block(rows):
        outputs = []
        for which in range(width // HEAD_DIM):
            start = which * HEAD_DIM
            stop = start + HEAD_DIM
            own = attend(rows[:, start:stop], head_k[:, start:stop], head_v[:, start:stop])
            other = attend(rows[:, start:stop], cross_k[:, start:stop], cross_v[:, start:stop])
            outputs.append((own + other).astype(jnp.bfloat16))
        return jnp.concatenate(outputs, axis=1)

    mixed_heads = lax.map(one_block, head_q.reshape(count // block, block, width)).reshape(
        1, count, width
    )
    returned = lax.all_to_all(
        as_sent(mixed_heads), "seq", split_axis=1, concat_axis=0, tiled=True
    ).astype(mixed_heads.dtype)
    attn_rows = (
        returned.reshape(ratio, 8, tokens // ratio, width)
        .transpose(0, 2, 1, 3)
        .reshape(tokens, dim)
    )
    projected = jnp.dot(attn_rows, w_out, preferred_element_type=jnp.float32)
    result = (hidden_in[0].astype(jnp.float32) + gate[0] * projected).astype(jnp.bfloat16)
    return result[None]


def solution(mesh):
    placed = (
        P("view", "seq", None),
        P("view", "seq", None),
        P("view", "seq", None),
        P("view", "seq", None),
        P("view", None),
        P(),
    )
    return jax.shard_map(
        body, mesh=mesh, in_specs=placed, out_specs=P("view", "seq", None), check_vma=False
    )
```

profile of v0, /device:TPU:2, one launch (start us, length us, event | category | flops | bytes accessed | tf_op | source)
XLA Modules:
  0.0 551.7 jit_solution(14247844305516351579)
XLA Ops:
  1.3 1.5 broadcast_in_dim.17
  2.8 10.1 %all-to-all-start.2 = ((bf16[32,128,192]{1,2,0:T(8,128)(2,1)}), bf16[32,128,192]{1,2,0:T(8,128)(2,1)S(1)}, u32[]{:S(2)}, u32[]{:S(2)}) async-start(bf16[32,128,192]{1,2,0:T(8,128)(2,1)} %bitcast.12), calls=%async_computation.2 | async-start | bytes 3145728 | tf_op jit(solution)/shard_map/all_to_all | solution.py:66
  14.1 36.7 %all-to-all-done.2 = bf16[32,128,192]{1,2,0:T(8,128)(2,1)S(1)} async-done(((bf16[32,128,192]{1,2,0:T(8,128)(2,1)}), bf16[32,128,192]{1,2,0:T(8,128)(2,1)S(1)}, u32[]{:S(2)}, u32[]{:S(2)}) %all-to-all-start.2) | async-done | bytes 1572896 | tf_op jit(solution)/shard_map/all_to_all | solution.py:66
  50.8 1.7 broadcast_in_dim.16
  52.5 5.8 %all-to-all-start.1 = ((bf16[32,128,192]{1,2,0:T(8,128)(2,1)}), bf16[32,128,192]{1,2,0:T(8,128)(2,1)S(1)}, u32[]{:S(2)}, u32[]{:S(2)}) async-start(bf16[32,128,192]{1,2,0:T(8,128)(2,1)} %bitcast.51), calls=%async_computation.1 | async-start | bytes 3145728 | tf_op jit(solution)/shard_map/all_to_all | solution.py:63
  59.4 2.3 reduce_sum.72
  62.7 44.2 %all-gather = bf16[256,1536]{1,0:T(8,128)(2,1)} all-gather(bf16[32,1536]{1,0:T(8,128)(2,1)S(1)} %multiply_convert_fusion.1), channel_id=2, replica_groups=mesh['view'=8,'seq'=32] {'view'}, dimensions={0}, use_global_device_ids=true | all-gather | bytes 884736 | tf_op jit(solution)/shard_map/all_gather | solution.py:56
  106.9 2.3 copy.42
  109.2 3.7 broadcast_in_dim.18
  112.9 10.3 %all-to-all-start.3 = ((bf16[32,256,192]{1,2,0:T(8,128)(2,1)}), bf16[32,256,192]{1,2,0:T(8,128)(2,1)S(1)}, u32[]{:S(2)}, u32[]{:S(2)}) async-start(bf16[32,256,192]{1,2,0:T(8,128)(2,1)} %bitcast.49), calls=%async_computation.3 | async-start | bytes 6291456 | tf_op jit(solution)/shard_map/all_to_all | solution.py:69
  124.4 1.6 reduce_sum.73
  126.0 45.0 %all-gather.1 = bf16[256,1536]{1,0:T(8,128)(2,1)} all-gather(bf16[32,1536]{1,0:T(8,128)(2,1)S(1)} %multiply_convert_fusion), channel_id=3, replica_groups=mesh['view'=8,'seq'=32] {'view'}, dimensions={0}, use_global_device_ids=true | all-gather | bytes 884736 | tf_op jit(solution)/shard_map/all_gather | solution.py:57
  171.0 2.3 copy.44
  173.3 21.4 %all-to-all-done.3 = bf16[32,256,192]{1,2,0:T(8,128)(2,1)S(1)} async-done(((bf16[32,256,192]{1,2,0:T(8,128)(2,1)}), bf16[32,256,192]{1,2,0:T(8,128)(2,1)S(1)}, u32[]{:S(2)}, u32[]{:S(2)}) %all-to-all-start.3) | async-done | bytes 3145760 | tf_op jit(solution)/shard_map/all_to_all | solution.py:69
  194.7 3.8 broadcast_in_dim.19
  198.5 7.6 %all-to-all-start.4 = ((bf16[32,256,192]{1,2,0:T(8,128)(2,1)}), bf16[32,256,192]{1,2,0:T(8,128)(2,1)}, u32[]{:S(2)}, u32[]{:S(2)}) async-start(bf16[32,256,192]{1,2,0:T(8,128)(2,1)} %bitcast.50), calls=%async_computation.4 | async-start | bytes 6291456 | tf_op jit(solution)/shard_map/all_to_all | solution.py:72
  207.3 2.0 copy.37
  209.3 68.3 %all-to-all-done.4 = bf16[32,256,192]{1,2,0:T(8,128)(2,1)} async-done(((bf16[32,256,192]{1,2,0:T(8,128)(2,1)}), bf16[32,256,192]{1,2,0:T(8,128)(2,1)}, u32[]{:S(2)}, u32[]{:S(2)}) %all-to-all-start.4) | async-done | bytes 3145760 | tf_op jit(solution)/shard_map/all_to_all | solution.py:72
  277.6 7.6 %all-to-all-start = ((bf16[32,32,192]{2,1,0:T(8,128)(2,1)}), bf16[32,32,192]{2,1,0:T(8,128)(2,1)}, u32[]{:S(2)}, u32[]{:S(2)}) async-start(bf16[32,32,192]{2,1,0:T(8,128)(2,1)} %bitcast.60), calls=%async_computation | async-start | bytes 1048576 | tf_op jit(solution)/shard_map/all_to_all | solution.py:62
  285.2 3.8 copy.54
  289.1 3.1 copy.53
  292.2 6.1 %copy.55 = bf16[32,256,192]{2,1,0:T(8,128)(2,1)} copy(bf16[32,256,192]{1,2,0:T(8,128)(2,1)} %copy-done.3) | data formatting | bytes 6291456 | tf_op jit(solution)/shard_map/while | solution.py:90
  298.3 6.1 %copy.56 = bf16[32,256,192]{2,1,0:T(8,128)(2,1)} copy(bf16[32,256,192]{1,2,0:T(8,128)(2,1)} %all-to-all-done.4) | data formatting | bytes 6291456 | tf_op jit(solution)/shard_map/while | solution.py:90
  304.4 212.4 %while.10 = (s32[]{:T(128)}, bf16[2,512,192]{1,2,0:T(8,128)(2,1)S(1)}, bf16[2,512,192]{2,1,0:T(8,128)(2,1)}, bf16[4096,192]{1,0:T(8,128)(2,1)S(1)}, bf16[4096,19...) while((s32[]{:T(128)}, bf16[2,512,192]{1,2,0:T(8,128)(2,1)S(1)}, ...), condition=%wide.region_15.16_spmd, body=%wide.region_2.15_spmd.sunk | while | flops 5002487808 | bytes 292024576 | solution.py:90
  327.8 8.6 %multiply_reduce_fusion.16 = (f32[512]{0:T(512)S(1)}, f32[512,8192]{1,0:T(8,128)}) fusion(bf16[8192,192]{1,0:T(8,128)(2,1)} %get-tuple-element.164, bf16[512,192]{1,0:T(8,128)(2,1)S(1)} %dynamic-slice_bitcast_fusion.2), kind=kOutput, calls=%fused_computation.8.clone.1 | convolution fusion | flops 545259008 | bytes 19007488 | tf_op jit(solution)/shard_map/while/body/eval_jaxpr/dot_general | solution.py:18
  336.4 8.6 %fusion.87 = f32[512]{0:T(512)S(1)} fusion(f32[512,8192]{1,0:T(8,128)} %get-tuple-element.139, f32[512]{0:T(512)S(1)} %get-tuple-element.140), kind=kLoop, calls=%fused_computation.9.clone.1 | loop fusion | flops 12582400 | bytes 16781312 | tf_op jit(solution)/shard_map/while/body/eval_jaxpr/reduce_sum | solution.py:21
  345.0 8.4 %fusion.88 = f32[512,64]{0,1:T(8,128)S(1)} fusion(f32[512,8192]{1,0:T(8,128)} %get-tuple-element.139, f32[512]{0:T(512)S(1)} %fusion.87, f32[512]{0:T(512)S(1)} %get-tuple-element.140, bf16[8192,192]{1,0:T(8,128)(2,1)} %get-tuple-element.165), kind=kOutput, calls=%fused_computation.18.clone.1 | convolution fusion | flops 553648128 | bytes 19009536 | tf_op jit(solution)/shard_map/while/body/eval_jaxpr/dot_general | solution.py:22
  353.4 1.3 multiply_reduce_fusion.17
  354.8 1.5 fusion.89
  356.3 2.1 fusion.90
  358.5 7.0 %multiply_reduce_fusion.14 = (f32[512]{0:T(512)S(1)}, f32[512,8192]{1,0:T(8,128)}) fusion(bf16[8192,192]{1,0:T(8,128)(2,1)S(1)} %copy-done, bf16[512,192]{1,0:T(8,128)(2,1)S(1)} %dynamic-slice_bitcast_fusion.2), kind=kOutput, calls=%fused_computation.7.clone.1 | convolution fusion | flops 545259008 | bytes 19007488 | tf_op jit(solution)/shard_map/while/body/eval_jaxpr/dot_general | solution.py:18
  365.5 8.6 %fusion.83 = f32[512]{0:T(512)S(1)} fusion(f32[512,8192]{1,0:T(8,128)} %get-tuple-element.135, f32[512]{0:T(512)S(1)} %get-tuple-element.136), kind=kLoop, calls=%fused_computation.10.clone.1 | loop fusion | flops 12582400 | bytes 16781312 | tf_op jit(solution)/shard_map/while/body/eval_jaxpr/reduce_sum | solution.py:21
  374.1 9.2 %fusion.84 = f32[512,64]{0,1:T(8,128)S(1)} fusion(f32[512,8192]{1,0:T(8,128)} %get-tuple-element.135, f32[512]{0:T(512)S(1)} %fusion.83, f32[512]{0:T(512)S(1)} %get-tuple-element.136, bf16[8192,192]{1,0:T(8,128)(2,1)} %get-tuple-element.165), kind=kOutput, calls=%fused_computation.19.clone.1 | convolution fusion | flops 553648128 | bytes 19009536 | tf_op jit(solution)/shard_map/while/body/eval_jaxpr/dot_general | solution.py:22
  383.3 2.8 multiply_reduce_fusion.15
  386.1 1.5 fusion.85
  387.6 2.3 fusion.86
  389.9 7.0 %multiply_reduce_fusion.12 = (f32[512]{0:T(512)S(1)}, f32[512,8192]{1,0:T(8,128)}) fusion(bf16[8192,192]{1,0:T(8,128)(2,1)S(1)} %copy-done, bf16[512,192]{1,0:T(8,128)(2,1)S(1)} %dynamic-slice_bitcast_fusion.2), kind=kOutput, calls=%fused_computation.6.clone.1 | convolution fusion | flops 545259008 | bytes 19007488 | tf_op jit(solution)/shard_map/while/body/eval_jaxpr/dot_general | solution.py:18
  396.9 8.6 %fusion.79 = f32[512]{0:T(512)S(1)} fusion(f32[512,8192]{1,0:T(8,128)} %get-tuple-element.131, f32[512]{0:T(512)S(1)} %get-tuple-element.132), kind=kLoop, calls=%fused_computation.11.clone.1 | loop fusion | flops 12582400 | bytes 16781312 | tf_op jit(solution)/shard_map/while/body/eval_jaxpr/reduce_sum | solution.py:21
  405.5 8.6 %fusion.80 = f32[512,64]{0,1:T(8,128)S(1)} fusion(f32[512,8192]{1,0:T(8,128)} %get-tuple-element.131, f32[512]{0:T(512)S(1)} %fusion.79, f32[512]{0:T(512)S(1)} %get-tuple-element.132, bf16[8192,192]{1,0:T(8,128)(2,1)} %get-tuple-element.165), kind=kOutput, calls=%fused_computation.20.clone.1 | convolution fusion | flops 553648128 | bytes 19009536 | tf_op jit(solution)/shard_map/while/body/eval_jaxpr/dot_general | solution.py:22
  414.1 1.3 multiply_reduce_fusion.13
  415.4 1.5 fusion.81
  417.0 2.1 fusion.82
  420.3 8.6 %multiply_reduce_fusion.16 = (f32[512]{0:T(512)S(1)}, f32[512,8192]{1,0:T(8,128)}) fusion(bf16[8192,192]{1,0:T(8,128)(2,1)} %get-tuple-element.164, bf16[512,192]{1,0:T(8,128)(2,1)S(1)} %dynamic-slice_bitcast_fusion.2), kind=kOutput, calls=%fused_computation.8.clone.1 | convolution fusion | flops 545259008 | bytes 19007488 | tf_op jit(solution)/shard_map/while/body/eval_jaxpr/dot_general | solution.py:18
  428.9 8.6 %fusion.87 = f32[512]{0:T(512)S(1)} fusion(f32[512,8192]{1,0:T(8,128)} %get-tuple-element.139, f32[512]{0:T(512)S(1)} %get-tuple-element.140), kind=kLoop, calls=%fused_computation.9.clone.1 | loop fusion | flops 12582400 | bytes 16781312 | tf_op jit(solution)/shard_map/while/body/eval_jaxpr/reduce_sum | solution.py:21
  437.5 8.4 %fusion.88 = f32[512,64]{0,1:T(8,128)S(1)} fusion(f32[512,8192]{1,0:T(8,128)} %get-tuple-element.139, f32[512]{0:T(512)S(1)} %fusion.87, f32[512]{0:T(512)S(1)} %get-tuple-element.140, bf16[8192,192]{1,0:T(8,128)(2,1)} %get-tuple-element.165), kind=kOutput, calls=%fused_computation.18.clone.1 | convolution fusion | flops 553648128 | bytes 19009536 | tf_op jit(solution)/shard_map/while/body/eval_jaxpr/dot_general | solution.py:22
  445.9 1.3 multiply_reduce_fusion.17
  447.3 1.5 fusion.89
  448.8 2.1 fusion.90
  451.0 7.0 %multiply_reduce_fusion.14 = (f32[512]{0:T(512)S(1)}, f32[512,8192]{1,0:T(8,128)}) fusion(bf16[8192,192]{1,0:T(8,128)(2,1)S(1)} %copy-done, bf16[512,192]{1,0:T(8,128)(2,1)S(1)} %dynamic-slice_bitcast_fusion.2), kind=kOutput, calls=%fused_computation.7.clone.1 | convolution fusion | flops 545259008 | bytes 19007488 | tf_op jit(solution)/shard_map/while/body/eval_jaxpr/dot_general | solution.py:18
  458.0 8.6 %fusion.83 = f32[512]{0:T(512)S(1)} fusion(f32[512,8192]{1,0:T(8,128)} %get-tuple-element.135, f32[512]{0:T(512)S(1)} %get-tuple-element.136), kind=kLoop, calls=%fused_computation.10.clone.1 | loop fusion | flops 12582400 | bytes 16781312 | tf_op jit(solution)/shard_map/while/body/eval_jaxpr/reduce_sum | solution.py:21
  466.6 9.2 %fusion.84 = f32[512,64]{0,1:T(8,128)S(1)} fusion(f32[512,8192]{1,0:T(8,128)} %get-tuple-element.135, f32[512]{0:T(512)S(1)} %fusion.83, f32[512]{0:T(512)S(1)} %get-tuple-element.136, bf16[8192,192]{1,0:T(8,128)(2,1)} %get-tuple-element.165), kind=kOutput, calls=%fused_computation.19.clone.1 | convolution fusion | flops 553648128 | bytes 19009536 | tf_op jit(solution)/shard_map/while/body/eval_jaxpr/dot_general | solution.py:22
  475.8 2.8 multiply_reduce_fusion.15
  478.6 1.5 fusion.85
  480.1 2.3 fusion.86
  482.4 7.0 %multiply_reduce_fusion.12 = (f32[512]{0:T(512)S(1)}, f32[512,8192]{1,0:T(8,128)}) fusion(bf16[8192,192]{1,0:T(8,128)(2,1)S(1)} %copy-done, bf16[512,192]{1,0:T(8,128)(2,1)S(1)} %dynamic-slice_bitcast_fusion.2), kind=kOutput, calls=%fused_computation.6.clone.1 | convolution fusion | flops 545259008 | bytes 19007488 | tf_op jit(solution)/shard_map/while/body/eval_jaxpr/dot_general | solution.py:18
  489.4 8.6 %fusion.79 = f32[512]{0:T(512)S(1)} fusion(f32[512,8192]{1,0:T(8,128)} %get-tuple-element.131, f32[512]{0:T(512)S(1)} %get-tuple-element.132), kind=kLoop, calls=%fused_computation.11.clone.1 | loop fusion | flops 12582400 | bytes 16781312 | tf_op jit(solution)/shard_map/while/body/eval_jaxpr/reduce_sum | solution.py:21
  498.0 8.6 %fusion.80 = f32[512,64]{0,1:T(8,128)S(1)} fusion(f32[512,8192]{1,0:T(8,128)} %get-tuple-element.131, f32[512]{0:T(512)S(1)} %fusion.79, f32[512]{0:T(512)S(1)} %get-tuple-element.132, bf16[8192,192]{1,0:T(8,128)(2,1)} %get-tuple-element.165), kind=kOutput, calls=%fused_computation.20.clone.1 | convolution fusion | flops 553648128 | bytes 19009536 | tf_op jit(solution)/shard_map/while/body/eval_jaxpr/dot_general | solution.py:22
  507.9 1.5 fusion.81
  509.4 2.1 fusion.82
  517.8 4.0 reduce.1
  521.8 1.3 reshape.113
  523.2 8.3 %all-to-all-start.5 = ((bf16[32,2,3072]{2,1,0:T(2,128)(2,1)}), bf16[32,2,3072]{2,1,0:T(2,128)(2,1)S(1)}, u32[]{:S(2)}, u32[]{:S(2)}) async-start(bf16[32,2,3072]{2,1,0:T(2,128)(2,1)} %reshape.113), calls=%async_computation.5 | async-start | bytes 786432 | tf_op jit(solution)/shard_map/all_to_all | solution.py:93
  531.5 14.5 %all-to-all-done.5 = bf16[32,2,3072]{2,1,0:T(2,128)(2,1)S(1)} async-done(((bf16[32,2,3072]{2,1,0:T(2,128)(2,1)}), bf16[32,2,3072]{2,1,0:T(2,128)(2,1)S(1)}, u32[]{:S(2)}, u32[]{:S(2)}) %all-to-all-start.5) | async-done | bytes 393248 | tf_op jit(solution)/shard_map/all_to_all | solution.py:93
  547.6 3.9 fusion.51
  (63 shorter events, 13.4 us)
Async XLA Ops:
  0.0 58.3 %copy-start.9 = (bf16[1,128,1536]{2,1,0:T(8,128)(2,1)S(1)}, bf16[1,128,1536]{2,1,0:T(8,128)(2,1)}, u32[]{:S(2)}) copy-start(bf16[1,128,1536]{2,1,0:T(8,128)(2,1)} %param.9) | copy-start | bytes 1179652
  2.8 48.0 %all-to-all-start.2 = ((bf16[32,128,192]{1,2,0:T(8,128)(2,1)}), bf16[32,128,192]{1,2,0:T(8,128)(2,1)S(1)}, u32[]{:S(2)}, u32[]{:S(2)}) async-start(bf16[32,128,192]{1,2,0:T(8,128)(2,1)} %bitcast.12), calls=%async_computation.2 | async-start | bytes 3145728 | tf_op jit(solution)/shard_map/all_to_all | solution.py:66
  50.8 62.1 %copy-start.4 = (bf16[32,128,192]{1,2,0:T(8,128)(2,1)}, bf16[32,128,192]{1,2,0:T(8,128)(2,1)S(1)}, u32[]{:S(2)}) copy-start(bf16[32,128,192]{1,2,0:T(8,128)(2,1)S(1)} %all-to-all-done.2) | copy-start | bytes 4718596
  52.5 56.7 %all-to-all-start.1 = ((bf16[32,128,192]{1,2,0:T(8,128)(2,1)}), bf16[32,128,192]{1,2,0:T(8,128)(2,1)S(1)}, u32[]{:S(2)}, u32[]{:S(2)}) async-start(bf16[32,128,192]{1,2,0:T(8,128)(2,1)} %bitcast.51), calls=%async_computation.1 | async-start | bytes 3145728 | tf_op jit(solution)/shard_map/all_to_all | solution.py:63
  59.4 63.8 %copy-start.10 = (bf16[1,128,1536]{2,1,0:T(8,128)(2,1)S(1)}, bf16[1,128,1536]{2,1,0:T(8,128)(2,1)}, u32[]{:S(2)}) copy-start(bf16[1,128,1536]{2,1,0:T(8,128)(2,1)} %param.10) | copy-start | bytes 1179652
  109.2 3.7 copy-start.5
  112.9 81.8 %all-to-all-start.3 = ((bf16[32,256,192]{1,2,0:T(8,128)(2,1)}), bf16[32,256,192]{1,2,0:T(8,128)(2,1)S(1)}, u32[]{:S(2)}, u32[]{:S(2)}) async-start(bf16[32,256,192]{1,2,0:T(8,128)(2,1)} %bitcast.49), calls=%async_computation.3 | async-start | bytes 6291456 | tf_op jit(solution)/shard_map/all_to_all | solution.py:69
  126.0 80.1 %copy-start.11 = (bf16[1,128,1536]{2,1,0:T(8,128)(2,1)S(1)}, bf16[1,128,1536]{2,1,0:T(8,128)(2,1)}, u32[]{:S(2)}) copy-start(bf16[1,128,1536]{2,1,0:T(8,128)(2,1)} %param.8) | copy-start | bytes 1179652
  194.7 90.5 %copy-start.3 = (bf16[32,256,192]{1,2,0:T(8,128)(2,1)}, bf16[32,256,192]{1,2,0:T(8,128)(2,1)S(1)}, u32[]{:S(2)}) copy-start(bf16[32,256,192]{1,2,0:T(8,128)(2,1)S(1)} %all-to-all-done.3) | copy-start | bytes 9437188
  198.5 79.1 %all-to-all-start.4 = ((bf16[32,256,192]{1,2,0:T(8,128)(2,1)}), bf16[32,256,192]{1,2,0:T(8,128)(2,1)}, u32[]{:S(2)}, u32[]{:S(2)}) async-start(bf16[32,256,192]{1,2,0:T(8,128)(2,1)} %bitcast.50), calls=%async_computation.4 | async-start | bytes 6291456 | tf_op jit(solution)/shard_map/all_to_all | solution.py:72
  277.6 26.8 %all-to-all-start = ((bf16[32,32,192]{2,1,0:T(8,128)(2,1)}), bf16[32,32,192]{2,1,0:T(8,128)(2,1)}, u32[]{:S(2)}, u32[]{:S(2)}) async-start(bf16[32,32,192]{2,1,0:T(8,128)(2,1)} %bitcast.60), calls=%async_computation | async-start | bytes 1048576 | tf_op jit(solution)/shard_map/all_to_all | solution.py:62
  304.4 227.1 %copy-start.13 = (f32[1,1536]{1,0:T(1,128)S(1)}, f32[1,1536]{1,0:T(1,128)}, u32[]{:S(2)}) copy-start(f32[1,1536]{1,0:T(1,128)} %param.12) | copy-start | bytes 18436
  326.6 26.8 %copy-start.1 = (bf16[4096,192]{1,0:T(8,128)(2,1)}, bf16[4096,192]{1,0:T(8,128)(2,1)S(1)}, u32[]{:S(2)}) copy-start(bf16[4096,192]{1,0:T(8,128)(2,1)S(1)} %get-tuple-element.162) | copy-start | bytes 4718596 | tf_op jit(solution)/shard_map/while
  353.4 2.9 copy-start.6
  356.3 2.2 copy-start
  383.3 4.3 copy-start.7
  405.5 8.6 %copy-start.2 = (bf16[4096,192]{1,0:T(8,128)(2,1)S(1)}, bf16[4096,192]{1,0:T(8,128)(2,1)}, u32[]{:S(2)}) copy-start(bf16[4096,192]{1,0:T(8,128)(2,1)} %copy-done.1) | copy-start | bytes 4718596 | tf_op jit(solution)/shard_map/while
  414.1 2.9 copy-start.8
  419.1 26.8 %copy-start.1 = (bf16[4096,192]{1,0:T(8,128)(2,1)}, bf16[4096,192]{1,0:T(8,128)(2,1)S(1)}, u32[]{:S(2)}) copy-start(bf16[4096,192]{1,0:T(8,128)(2,1)S(1)} %get-tuple-element.162) | copy-start | bytes 4718596 | tf_op jit(solution)/shard_map/while
  445.9 2.9 copy-start.6
  448.8 2.2 copy-start
  475.8 4.3 copy-start.7
  498.0 8.6 %copy-start.2 = (bf16[4096,192]{1,0:T(8,128)(2,1)S(1)}, bf16[4096,192]{1,0:T(8,128)(2,1)}, u32[]{:S(2)}) copy-start(bf16[4096,192]{1,0:T(8,128)(2,1)} %copy-done.1) | copy-start | bytes 4718596 | tf_op jit(solution)/shard_map/while
  506.6 2.9 copy-start.8
  516.8 30.8 %copy-start.12 = (bf16[1,128,1536]{2,1,0:T(8,128)(2,1)S(1)}, bf16[1,128,1536]{2,1,0:T(8,128)(2,1)}, u32[]{:S(2)}) copy-start(bf16[1,128,1536]{2,1,0:T(8,128)(2,1)} %param.11) | copy-start | bytes 1179652
  523.2 22.8 %all-to-all-start.5 = ((bf16[32,2,3072]{2,1,0:T(2,128)(2,1)}), bf16[32,2,3072]{2,1,0:T(2,128)(2,1)S(1)}, u32[]{:S(2)}, u32[]{:S(2)}) async-start(bf16[32,2,3072]{2,1,0:T(2,128)(2,1)} %reshape.113), calls=%async_computation.5 | async-start | bytes 786432 | tf_op jit(solution)/shard_map/all_to_all | solution.py:93
where the time goes:
time: 560 us; the launch traced here: 552 us
  waiting for transfers between devices  141 us (25%)
  matrix products  125 us (22%)
  blocking collectives  89.2 us (16%)
  other arithmetic  69.7 us (12%)
  starting transfers between devices  49.6 us (9%)
  local copies, waits for them, and re-layouts  48.9 us (9%)
  loops' own time  27.7 us (5%)
    all_to_all x1, waiting for transfers between devices, body(): lax.all_to_all(copied_items(pooled_v, ratio), 'seq', split_axis=0, concat...  68.3 us
    dot_general x12, matrix products, attend(): jnp.dot(weights.astype(jnp.bfloat16), valueset, preferred_element_type=jn...  65.3 us
    reduce_sum x12, other arithmetic, attend(): weights = weights / jnp.sum(weights, axis=-1, keepdims=True)  60.7 us
    dot_general x12, matrix products, attend(): jnp.dot(query, keyset.T, preferred_element_type=jnp.float32)  56.1 us
    all_gather x1, blocking collectives, body(): lax.all_gather(pool_rows(local_v)[None], 'view', axis=0, tiled=True)  45 us
    all_gather x1, blocking collectives, body(): lax.all_gather(pool_rows(local_k)[None], 'view', axis=0, tiled=True)  44.2 us
    all_to_all x1, waiting for transfers between devices, body(): lax.all_to_all(copied_items(local_v, ratio), 'seq', split_axis=0, concat_...  36.7 us
    another operation x1, loops' own time, body(): lax.map(one_block, head_q.reshape(count // block, block, width))  27.7 us
  transfers between devices with their start and end apart: 6, of which 4 were waited for; matrix products, arithmetic and copies ran while one was open for 6% of the time, Pallas kernels for 0%

commit v1 on v0

v1 whole, which is shorter than its diff:
```python
import functools
import math

import jax
import jax.numpy as jnp
from jax import lax
from jax.experimental import pallas as pl
from jax.experimental.pallas import tpu as pltpu
from jax.sharding import Mesh, PartitionSpec as P

EXP2_SCALE = math.log2(math.e) / 8.0
VMEM = 56 * 2**20
AXES = ("y", "xh", "xl", "z", "core")
SIZES = (4, 2, 2, 8, 2)


def swap_halves(tile):
    return jnp.concatenate([tile[:, 64:], tile[:, :64]], axis=1)


def pair_heads(tile):
    half = tile.shape[0] // 2
    upper, lower = tile[:half], tile[half:]
    first = jnp.concatenate([upper[:, :64], lower[:, :64]], axis=1)
    second = jnp.concatenate([upper[:, 64:], lower[:, 64:]], axis=1)
    return first, second


def prep_kernel(q_ref, k_ref, v_ref, pool_ref, own_ref):
    rows = lax.broadcasted_iota(jnp.int32, (32, 128), 0)
    cols = lax.broadcasted_iota(jnp.int32, (32, 128), 1)
    mean4 = jnp.where(cols // 4 == rows, 0.25, 0.0).astype(jnp.bfloat16)
    for j in range(12):
        span = pl.ds(j * 128, 128)
        q, k, v = q_ref[:, span], k_ref[:, span], v_ref[:, span]
        qt, vt = q.T, v.T
        packed_k = pair_heads(k)
        pooled_k = pair_heads(
            jnp.dot(mean4, k, preferred_element_type=jnp.float32).astype(jnp.bfloat16)
        )
        pooled_v = pair_heads(
            jnp.dot(mean4, v, preferred_element_type=jnp.float32).astype(jnp.bfloat16)
        )
        for side in range(2):
            group, member = divmod(2 * j + side, 3)
            own_ref[group, 0, member] = qt[side * 64 : side * 64 + 64]
            own_ref[group, 1, member] = packed_k[side]
            own_ref[group, 2, member] = vt[side * 64 : side * 64 + 64]
            pool_ref[group, 0, member] = pooled_k[side]
            pool_ref[group, 1, member] = pooled_v[side]


def prep(q, k, v):
    return pl.pallas_call(
        prep_kernel,
        out_shape=(
            jax.ShapeDtypeStruct((8, 2, 3, 16, 128), jnp.bfloat16),
            jax.ShapeDtypeStruct((8, 3, 3, 64, 128), jnp.bfloat16),
        ),
        compiler_params=pltpu.CompilerParams(vmem_limit_bytes=VMEM),
        name="prep",
    )(q, k, v)


def repack_kernel(pool_ref, out_ref):
    for member in range(3):
        out_ref[member, 0] = pool_ref[:, 0, member].reshape(128, 128)
        out_ref[member, 1] = pool_ref[:, 1, member].reshape(128, 128).T


def repack(pool):
    return pl.pallas_call(
        repack_kernel,
        out_shape=jax.ShapeDtypeStruct((3, 2, 128, 128), jnp.bfloat16),
        name="repack",
    )(pool)


def own_tile(ref, tile):
    keys = ref[2 * tile : 2 * tile + 2, 0].reshape(128, 128)
    values = jnp.concatenate([ref[2 * tile, 1], ref[2 * tile + 1, 1]], axis=1)
    return keys, values


def own_order(p):
    return jnp.concatenate([p[0:64], p[128:192], p[64:128], p[192:256]], axis=0)


def pool_tile(ref, tile):
    both = ref[tile, 1]
    return ref[tile, 0], jnp.concatenate([both[:64], both[64:]], axis=1)


def pool_order(p):
    return p


def attend_kernel(count, tile_of, order, with_base, *refs):
    q_ref, kv_refs, rest = refs[0], refs[1 : 1 + count], refs[1 + count :]
    if with_base:
        base_ref, out_ref, s0, s1 = rest
    else:
        out_ref, s0, s1 = rest
    tiles = s0.shape[0]
    qt = jnp.concatenate([q_ref[0], q_ref[1]], axis=1)
    zero = jnp.zeros_like(qt)
    upper = jnp.concatenate([qt, zero], axis=0)
    lower = jnp.concatenate([zero, qt], axis=0)
    ones = jnp.ones((16, 256), jnp.bfloat16)

    def scores(ref, held):
        top = None
        for t in range(tiles):
            keys, _ = tile_of(ref, t)
            a = jnp.dot(keys, upper, preferred_element_type=jnp.float32)
            b = jnp.dot(keys, lower, preferred_element_type=jnp.float32)
            held[t, 0:128, :] = a
            held[t, 128:256, :] = b
            both = jnp.maximum(
                jnp.max(a.reshape(16, 8, 256), axis=0), jnp.max(b.reshape(16, 8, 256), axis=0)
            )
            top = both if top is None else jnp.maximum(top, both)
        return jnp.max(top, axis=0, keepdims=True)

    def weigh(ref, held, top, total):
        for t in range(tiles):
            _, values = tile_of(ref, t)
            p = jnp.exp2((held[t] - top) * EXP2_SCALE).astype(jnp.bfloat16)
            total = total + jnp.dot(
                jnp.concatenate([values, ones], axis=0),
                order(p),
                preferred_element_type=jnp.float32,
            )
        return total

    slots = (s0, s1)
    following = scores(kv_refs[0], s0)
    top, total = following, jnp.zeros((80, 256), jnp.float32)
    for b in range(count):
        newer = jnp.maximum(top, following)
        if b:
            total = total * jnp.exp2((top - newer) * EXP2_SCALE)
        top = newer
        if b + 1 < count:
            following = scores(kv_refs[b + 1], slots[(b + 1) % 2])
        total = weigh(kv_refs[b], slots[b % 2], top, total)
    result = total[0:64] / total[64:65]
    if with_base:
        result = (result + base_ref[...]).astype(jnp.bfloat16)
        out_ref[0] = result[:, :128]
        out_ref[1] = result[:, 128:]
    else:
        out_ref[...] = result


def attend(own, kvs, tile_of, order, tiles, base, name):
    count = len(kvs)
    in_specs = [pl.BlockSpec((2, None, None, 64, 128), lambda h, i: (i, 0, h, 0, 0))]
    for kv, at in kvs:
        shape = kv.shape
        if at == 2:
            in_specs.append(
                pl.BlockSpec((shape[0], shape[1], None, 64, 128), lambda h, i: (0, 0, h, 0, 0))
            )
        else:
            in_specs.append(
                pl.BlockSpec((shape[0], None, 2, 128, 128), lambda h, i: (0, h, 0, 0, 0))
            )
    args = [own] + [kv for kv, _ in kvs]
    if base is not None:
        args.append(base)
        in_specs.append(pl.BlockSpec((None, 64, 256), lambda h, i: (h, 0, i)))
        out_spec = pl.BlockSpec((2, None, 64, 128), lambda h, i: (i, h, 0, 0))
        out_shape = jax.ShapeDtypeStruct((8, 3, 64, 128), jnp.bfloat16)
    else:
        out_spec = pl.BlockSpec((None, 64, 256), lambda h, i: (h, 0, i))
        out_shape = jax.ShapeDtypeStruct((3, 64, 1024), jnp.float32)
    return pl.pallas_call(
        functools.partial(attend_kernel, count, tile_of, order, base is not None),
        grid=(3, 4),
        in_specs=in_specs,
        out_specs=out_spec,
        out_shape=out_shape,
        scratch_shapes=[pltpu.VMEM((tiles, 256, 256), jnp.float32)] * 2,
        compiler_params=pltpu.CompilerParams(vmem_limit_bytes=VMEM),
        name=name,
    )(*args)


def project_kernel(heads_ref, w_ref, hidden_ref, gate_ref, out_ref):
    projected = lax.dot_general(
        heads_ref[...], w_ref[...], (((0,), (0,)), ((), ())), preferred_element_type=jnp.float32
    )
    out_ref[...] = (hidden_ref[...].astype(jnp.float32) + gate_ref[...] * projected).astype(
        jnp.bfloat16
    )


def project(heads, w_out, hidden, gate):
    width = 512
    return pl.pallas_call(
        project_kernel,
        grid=(1536 // width,),
        in_specs=[
            pl.BlockSpec((1536, 128), lambda n: (0, 0)),
            pl.BlockSpec((1536, width), lambda n: (0, n)),
            pl.BlockSpec((128, width), lambda n: (0, n)),
            pl.BlockSpec((1, width), lambda n: (0, n)),
        ],
        out_specs=pl.BlockSpec((128, width), lambda n: (0, n)),
        out_shape=jax.ShapeDtypeStruct((128, 1536), jnp.bfloat16),
        compiler_params=pltpu.CompilerParams(vmem_limit_bytes=VMEM),
        name="project",
    )(heads, w_out, hidden, gate)


def shifted(array, axis, size, step):
    return lax.ppermute(array, axis, [(i, (i + step) % size) for i in range(size)])


def body(queries, keys, values, hidden_in, gate, w_out):
    pool, own = prep(queries[0], keys[0], values[0])
    pool = lax.all_to_all(pool, "z", 0, 0, tiled=True)
    own = lax.all_to_all(own, "z", 0, 0, tiled=True)
    piece = repack(pool)
    x = ("xh", "xl")
    row = jnp.stack([piece] + [shifted(piece, x, 4, step) for step in (1, 3, 2)])
    plane = [row] + [shifted(row, "y", 4, step) for step in (1, 3, 2)]
    crossed = plane + [shifted(part, "core", 2, 1) for part in plane]
    kv = own[:, 1:]
    kv_x = shifted(kv, "xl", 2, 1)
    column = [kv, shifted(kv, "core", 2, 1), kv_x, shifted(kv_x, "core", 2, 1)]
    base = attend(own, [(part, 2) for part in column], own_tile, own_order, 4, None, "own")
    heads = attend(own, [(part, 1) for part in crossed], pool_tile, pool_order, 4, base, "cross")
    returned = lax.all_to_all(heads, "z", 0, 0, tiled=True)
    result = project(returned.reshape(1536, 128), w_out, hidden_in[0], gate)
    return result[None]


def solution(mesh):
    fine = Mesh(mesh.devices.reshape(SIZES), AXES)
    tokens = P(("y", "xh"), ("xl", "z", "core"), None)
    placed = (tokens, tokens, tokens, tokens, P(("y", "xh"), None), P())
    return jax.shard_map(body, mesh=fine, in_specs=placed, out_specs=tokens, check_vma=False)
```

time: 560 us -> 169 us (0.30); the launches traced: 552 us -> 167 us
  matrix products: 125 us -> 0 us
  waiting for transfers between devices: 141 us -> 39.2 us
  Pallas kernels: 0 us -> 70.2 us
  other arithmetic: 69.7 us -> 1.03 us
  blocking collectives: 89.2 us -> 38.7 us
  local copies, waits for them, and re-layouts: 48.9 us -> 1.62 us
  starting transfers between devices: 49.6 us -> 15.6 us
  loops' own time: 27.7 us -> 0 us
    all_to_all x6 -> x1, waiting for transfers between devices: 141 us -> 13.1 us  [body(): own = lax.all_to_all(own, 'z', 0, 0, tiled=True)]
    dot_general x25 -> x0, matrix products: 125 us -> none  [the longest x12 65.3 us: attend(): jnp.dot(weights.astype(jnp.bfloat16), valueset, preferred_element_type=jn...]
    all_gather x2 -> x0, blocking collectives: 89.2 us -> none  [the longest x1 45 us: body(): lax.all_gather(pool_rows(local_v)[None], 'view', axis=0, tiled=True)]
    pallas_call x0 -> x5, Pallas kernels: none -> 70.2 us  [the longest x2 61 us: attend(): pl.pallas_call(functools.partial(attend_kernel, count, tile_of, order, ba...]
    reduce_sum x14 -> x0, other arithmetic: 64.6 us -> none  [the longest x12 60.7 us: attend(): weights = weights / jnp.sum(weights, axis=-1, keepdims=True)]
    all_to_all x6 -> x1, starting transfers between devices: 49.6 us -> 3.56 us  [body(): own = lax.all_to_all(own, 'z', 0, 0, tiled=True)]
    all_to_all x0 -> x2, blocking collectives: none -> 38.7 us  [the longest x1 19.7 us: body(): returned = lax.all_to_all(heads, 'z', 0, 0, tiled=True)]
    another operation x1 -> x0, loops' own time: 27.7 us -> none  [body(): lax.map(one_block, head_q.reshape(count // block, block, width))]
  transfers between devices with their start and end apart: 6 -> 14, of which waited for: 4 -> 7; matrix products, arithmetic and copies ran while one was open for 6% -> 1% of each run, Pallas kernels for 0% -> 14%
where the time goes in v1:
time: 169 us; the launch traced here: 167 us
  Pallas kernels  70.2 us (42%)
  waiting for transfers between devices  39.2 us (23%)
  blocking collectives  38.7 us (23%)
  starting transfers between devices  15.6 us (9%)
    pallas_call x2, Pallas kernels, attend(): pl.pallas_call(functools.partial(attend_kernel, count, tile_of, order, ba...  61 us
    ppermute x13, waiting for transfers between devices, shifted(): lax.ppermute(array, axis, [(i, (i + step) % size) for i in range(size)])  26.1 us
    all_to_all x1, blocking collectives, body(): returned = lax.all_to_all(heads, 'z', 0, 0, tiled=True)  19.7 us
    all_to_all x1, blocking collectives, body(): pool = lax.all_to_all(pool, 'z', 0, 0, tiled=True)  19 us
    all_to_all x1, waiting for transfers between devices, body(): own = lax.all_to_all(own, 'z', 0, 0, tiled=True)  13.1 us
    ppermute x13, starting transfers between devices, shifted(): lax.ppermute(array, axis, [(i, (i + step) % size) for i in range(size)])  12.1 us
    pallas_call x1, Pallas kernels, project(): pl.pallas_call(project_kernel, grid=(1536 // width,), in_specs=[pl.BlockS...  4.66 us
    all_to_all x1, starting transfers between devices, body(): own = lax.all_to_all(own, 'z', 0, 0, tiled=True)  3.56 us
  transfers between devices with their start and end apart: 14, of which 7 were waited for; matrix products, arithmetic and copies ran while one was open for 1% of the time, Pallas kernels for 14%

profile of v1, /device:TPU:2, one launch (start us, length us, event | category | flops | bytes accessed | tf_op | source)
XLA Modules:
  0.0 166.5 jit_solution(18343726298358062202)
XLA Ops:
  0.0 2.8 %prep.1 = (bf16[8,2,3,16,128]{4,3,2,1,0:T(8,128)(2,1)}, bf16[8,3,3,64,128]{4,3,2,1,0:T(8,128)(2,1)}) custom-call(bf16[128,1536]{1,0:T(8,128)(2,1)} %bitcast.13, bf16[128,1536]{1,0:T(8,128)(2,1)} %bitcast.14, bf16[128,1536]{1,0:T(8,128)(2,1)} %bitcast.15), custom_call_target="tpu_custom_call" | custom-call | tf_op jit(solution)/shard_map/prep/pallas_call | solution.py:54
  2.9 19.0 %all_to_all.15.pool_ref = bf16[8,2,3,16,128]{4,3,2,1,0:T(8,128)(2,1)} all-to-all(bf16[8,2,3,16,128]{4,3,2,1,0:T(8,128)(2,1)} %get-tuple-element.8), channel_id=1, replica_groups=mesh['y'=4,'xh'=2,'xl'=2,'z'=8,'core'=2] {'z'}, dimensions={0} | all-to-all | bytes 393216 | tf_op jit(solution)/shard_map/all_to_all | solution.py:223
  21.9 3.6 %all-to-all-start = ((bf16[8,3,3,64,128]{4,3,2,1,0:T(8,128)(2,1)}), bf16[8,3,3,64,128]{4,3,2,1,0:T(8,128)(2,1)S(1)}, u32[]{:S(2)}, u32[]{:S(2)}) async-start(bf16[8,3,3,64,128]{4,3,2,1,0:T(8,128)(2,1)} %get-tuple-element.7), calls=%async_computation | async-start | bytes 2359296 | tf_op jit(solution)/shard_map/all_to_all | solution.py:224
  25.5 1.7 %repack.1 = bf16[3,2,128,128]{3,2,1,0:T(8,128)(2,1)} custom-call(bf16[8,2,3,16,128]{4,3,2,1,0:T(8,128)(2,1)} %all_to_all.15.pool_ref), custom_call_target="tpu_custom_call" | custom-call | tf_op jit(solution)/shard_map/repack/pallas_call | solution.py:72
  27.2 2.1 %collective-permute-start.2 = (bf16[3,2,128,128]{3,2,1,0:T(8,128)(2,1)}, bf16[3,2,128,128]{3,2,1,0:T(8,128)(2,1)S(1)}, u32[]{:S(2)}, u32[]{:S(2)}) collective-permute-start(bf16[3,2,128,128]{3,2,1,0:T(8,128)(2,1)} %repack.1), channel_id=1, source_target_pairs={{0,32},{16,48},{32,0},{48,16},{1,33},{17,49},{33,1},{49,17},{2,34}... | collective-permute-start | bytes 589832 | tf_op jit(solution)/shard_map/ppermute | solution.py:218
  29.3 1.4 collective-permute-start.1
  30.7 0.6 collective-permute-start
  31.3 4.5 %collective-permute-done.2 = bf16[3,2,128,128]{3,2,1,0:T(8,128)(2,1)S(1)} collective-permute-done((bf16[3,2,128,128]{3,2,1,0:T(8,128)(2,1)}, bf16[3,2,128,128]{3,2,1,0:T(8,128)(2,1)S(1)}, u32[]{:S(2)}, u32[]{:S(2)}) %collective-permute-start.2) | collective-permute-done | bytes 196640 | tf_op jit(solution)/shard_map/ppermute | solution.py:218
  35.8 2.0 %collective-permute-done.1 = bf16[3,2,128,128]{3,2,1,0:T(8,128)(2,1)S(1)} collective-permute-done((bf16[3,2,128,128]{3,2,1,0:T(8,128)(2,1)}, bf16[3,2,128,128]{3,2,1,0:T(8,128)(2,1)S(1)}, u32[]{:S(2)}, u32[]{:S(2)}) %collective-permute-start.1) | collective-permute-done | bytes 196640 | tf_op jit(solution)/shard_map/ppermute | solution.py:218
  37.8 0.1 collective-permute-done
  37.9 1.0 pad_maximum_fusion.refs_1_
  38.9 0.0 copy-start.1
  38.9 3.3 %collective-permute-start.5 = (bf16[4,3,2,128,128]{4,3,2,1,0:T(8,128)(2,1)S(1)}, bf16[4,3,2,128,128]{4,3,2,1,0:T(8,128)(2,1)S(1)}, u32[]{:S(2)}, u32[]{:S(2)}) collective-permute-start(bf16[4,3,2,128,128]{4,3,2,1,0:T(8,128)(2,1)S(1)} %pad_maximum_fusion.refs_1_), channel_id=1, source_target_pairs={{0,128},{64,192},{128,0},{192,64},{1,129},{65,193},{129,1},{193,65... | collective-permute-start | bytes 2359304 | tf_op jit(solution)/shard_map/ppermute | solution.py:218
  42.2 13.1 %all-to-all-done.refs_0_ = bf16[8,3,3,64,128]{4,3,2,1,0:T(8,128)(2,1)S(1)} async-done(((bf16[8,3,3,64,128]{4,3,2,1,0:T(8,128)(2,1)}), bf16[8,3,3,64,128]{4,3,2,1,0:T(8,128)(2,1)S(1)}, u32[]{:S(2)}, u32[]{:S(2)}) %all-to-all-start) | async-done | bytes 1179680 | tf_op jit(solution)/shard_map/all_to_all | solution.py:224
  55.3 0.0 copy-start
  55.3 0.1 slice.4.refs_1_
  55.3 0.0 copy-start.2
  55.3 0.6 collective-permute-start.11
  56.0 3.0 %collective-permute-start.4 = (bf16[4,3,2,128,128]{4,3,2,1,0:T(8,128)(2,1)S(1)}, bf16[4,3,2,128,128]{4,3,2,1,0:T(8,128)(2,1)S(1)}, u32[]{:S(2)}, u32[]{:S(2)}) collective-permute-start(bf16[4,3,2,128,128]{4,3,2,1,0:T(8,128)(2,1)S(1)} %pad_maximum_fusion.refs_1_), channel_id=1, source_target_pairs={{0,192},{64,0},{128,64},{192,128},{1,193},{65,1},{129,65},{193,129... | collective-permute-start | bytes 2359304 | tf_op jit(solution)/shard_map/ppermute | solution.py:218
  59.0 0.0 collective-permute-start.3
  59.0 0.0 collective-permute-start.10
  59.0 0.0 collective-permute-done.5.refs_4_
  59.0 0.0 copy-start.3
  59.0 0.5 collective-permute-start.6
  59.5 15.3 %collective-permute-done.11.refs_3_ = bf16[8,2,3,64,128]{4,3,2,1,0:T(8,128)(2,1)S(1)} collective-permute-done((bf16[8,2,3,64,128]{4,3,2,1,0:T(8,128)(2,1)S(1)}, bf16[8,2,3,64,128]{4,3,2,1,0:T(8,128)(2,1)S(1)}, u32[]{:S(2)}, u32[]{:S(2)}) %collective-permute-start.11) | collective-permute-done | bytes 786464 | tf_op jit(solution)/shard_map/ppermute | solution.py:218
  74.8 0.0 copy-start.7
  74.8 0.0 collective-permute-start.12
  74.8 1.0 collective-permute-done.4.refs_3_
  75.8 0.0 copy-start.4
  75.8 0.0 collective-permute-start.9
  75.8 3.2 %collective-permute-done.3.refs_2_ = bf16[4,3,2,128,128]{4,3,2,1,0:T(8,128)(2,1)S(1)} collective-permute-done((bf16[4,3,2,128,128]{4,3,2,1,0:T(8,128)(2,1)S(1)}, bf16[4,3,2,128,128]{4,3,2,1,0:T(8,128)(2,1)S(1)}, u32[]{:S(2)}, u32[]{:S(2)}) %collective-permute-start.3) | collective-permute-done | bytes 786464 | tf_op jit(solution)/shard_map/ppermute | solution.py:218
  79.0 0.0 copy-start.5
  79.0 0.0 collective-permute-start.8
  79.0 0.0 collective-permute-done.10.refs_2_
  79.0 0.0 copy-start.8
  79.0 0.5 collective-permute-start.7
  79.5 0.0 collective-permute-done.12.refs_4_
  79.5 0.0 copy-done
  79.6 0.0 copy-done.2
  79.6 0.0 copy-done.7
  79.6 0.4 copy-done.8
  80.0 22.1 %own.1.refs_9_ = f32[3,64,1024]{2,1,0:T(8,128)} custom-call(bf16[8,3,3,64,128]{4,3,2,1,0:T(8,128)(2,1)} %copy-done, bf16[8,2,3,64,128]{4,3,2,1,0:T(8,128)(2,1)} %copy-done.2, bf16[8,2,3,64,128]{4,3,2,1,0:T(8,128)(2,1)} %copy-done.8, bf16[8,2,3,64,128]{4,3,2,1,0:T(8,128)(2,1)} %copy-done.7, bf16[8,2,3,64,128]{4,3,2,1,0:T(8,128)(2,1)} %collective-permute-done.12.refs_4_), custom_call_target="tpu_custom_call" | custom-call | tf_op jit(solution)/shard_map/own/pallas_call | solution.py:178
  102.0 0.0 copy-done.3
  102.0 0.0 copy-done.4
  102.0 0.0 copy-done.5
  102.1 0.0 collective-permute-done.6.refs_5_
  102.1 0.0 copy-start.6
  102.1 0.0 collective-permute-done.9.refs_8_
  102.1 0.0 copy-start.9
  102.1 0.0 collective-permute-done.8.refs_7_
  102.1 0.0 collective-permute-done.7.refs_6_
  102.1 0.0 copy-done.1
  102.1 0.8 copy-done.6
  102.9 0.3 copy-done.9
  103.3 38.9 %cross.1 = bf16[8,3,64,128]{3,2,1,0:T(8,128)(2,1)} custom-call(bf16[8,3,3,64,128]{4,3,2,1,0:T(8,128)(2,1)} %copy-done, bf16[4,3,2,128,128]{4,3,2,1,0:T(8,128)(2,1)} %copy-done.1, bf16[4,3,2,128,128]{4,3,2,1,0:T(8,128)(2,1)} %copy-done.5, bf16[4,3,2,128,128]{4,3,2,1,0:T(8,128)(2,1)} %copy-done.4, bf16[4,3,2,128,128]{4,3,2,1,0:T(8,128)(2,1)} %copy-done.3, ...), custom_call_target="tpu_custom_call" | custom-call | tf_op jit(solution)/shard_map/cross/pallas_call | solution.py:178
  142.2 19.7 %all_to_all.16 = bf16[8,3,64,128]{3,2,1,0:T(8,128)(2,1)} all-to-all(bf16[8,3,64,128]{3,2,1,0:T(8,128)(2,1)} %cross.1), channel_id=1, replica_groups=mesh['y'=4,'xh'=2,'xl'=2,'z'=8,'core'=2] {'z'}, dimensions={0} | all-to-all | bytes 786432 | tf_op jit(solution)/shard_map/all_to_all | solution.py:235
  161.9 4.7 %project.1 = bf16[128,1536]{1,0:T(8,128)(2,1)} custom-call(bf16[1536,128]{1,0:T(8,128)(2,1)} %bitcast.10, bf16[1536,1536]{1,0:T(8,128)(2,1)} %w_ref.1, bf16[128,1536]{1,0:T(8,128)(2,1)} %bitcast.12, f32[1,1536]{1,0:T(1,128)} %gate_ref.1), custom_call_target="tpu_custom_call" | custom-call | tf_op jit(solution)/shard_map/project/pallas_call | solution.py:201
Async XLA Ops:
  21.9 33.4 %all-to-all-start = ((bf16[8,3,3,64,128]{4,3,2,1,0:T(8,128)(2,1)}), bf16[8,3,3,64,128]{4,3,2,1,0:T(8,128)(2,1)S(1)}, u32[]{:S(2)}, u32[]{:S(2)}) async-start(bf16[8,3,3,64,128]{4,3,2,1,0:T(8,128)(2,1)} %get-tuple-element.7), calls=%async_computation | async-start | bytes 2359296 | tf_op jit(solution)/shard_map/all_to_all | solution.py:224
  27.2 8.7 %collective-permute-start.2 = (bf16[3,2,128,128]{3,2,1,0:T(8,128)(2,1)}, bf16[3,2,128,128]{3,2,1,0:T(8,128)(2,1)S(1)}, u32[]{:S(2)}, u32[]{:S(2)}) collective-permute-start(bf16[3,2,128,128]{3,2,1,0:T(8,128)(2,1)} %repack.1), channel_id=1, source_target_pairs={{0,32},{16,48},{32,0},{48,16},{1,33},{17,49},{33,1},{49,17},{2,34}... | collective-permute-start | bytes 589832 | tf_op jit(solution)/shard_map/ppermute | solution.py:218
  29.3 8.5 %collective-permute-start.1 = (bf16[3,2,128,128]{3,2,1,0:T(8,128)(2,1)}, bf16[3,2,128,128]{3,2,1,0:T(8,128)(2,1)S(1)}, u32[]{:S(2)}, u32[]{:S(2)}) collective-permute-start(bf16[3,2,128,128]{3,2,1,0:T(8,128)(2,1)} %repack.1), channel_id=1, source_target_pairs={{0,48},{16,0},{32,16},{48,32},{1,49},{17,1},{33,17},{49,33},{2,50}... | collective-permute-start | bytes 589832 | tf_op jit(solution)/shard_map/ppermute | solution.py:218
  30.7 7.1 %collective-permute-start = (bf16[3,2,128,128]{3,2,1,0:T(8,128)(2,1)}, bf16[3,2,128,128]{3,2,1,0:T(8,128)(2,1)S(1)}, u32[]{:S(2)}, u32[]{:S(2)}) collective-permute-start(bf16[3,2,128,128]{3,2,1,0:T(8,128)(2,1)} %repack.1), channel_id=1, source_target_pairs={{0,16},{16,32},{32,48},{48,0},{1,17},{17,33},{33,49},{49,1},{2,18}... | collective-permute-start | bytes 589832 | tf_op jit(solution)/shard_map/ppermute | solution.py:218
  38.9 63.2 %copy-start.1 = (bf16[4,3,2,128,128]{4,3,2,1,0:T(8,128)(2,1)}, bf16[4,3,2,128,128]{4,3,2,1,0:T(8,128)(2,1)S(1)}, u32[]{:S(2)}) copy-start(bf16[4,3,2,128,128]{4,3,2,1,0:T(8,128)(2,1)S(1)} %pad_maximum_fusion.refs_1_) | copy-start | bytes 2359300
  38.9 20.1 %collective-permute-start.5 = (bf16[4,3,2,128,128]{4,3,2,1,0:T(8,128)(2,1)S(1)}, bf16[4,3,2,128,128]{4,3,2,1,0:T(8,128)(2,1)S(1)}, u32[]{:S(2)}, u32[]{:S(2)}) collective-permute-start(bf16[4,3,2,128,128]{4,3,2,1,0:T(8,128)(2,1)S(1)} %pad_maximum_fusion.refs_1_), channel_id=1, source_target_pairs={{0,128},{64,192},{128,0},{192,64},{1,129},{65,193},{129,1},{193,65... | collective-permute-start | bytes 2359304 | tf_op jit(solution)/shard_map/ppermute | solution.py:218
  55.3 24.3 %copy-start = (bf16[8,3,3,64,128]{4,3,2,1,0:T(8,128)(2,1)}, bf16[8,3,3,64,128]{4,3,2,1,0:T(8,128)(2,1)S(1)}, u32[]{:S(2)}) copy-start(bf16[8,3,3,64,128]{4,3,2,1,0:T(8,128)(2,1)S(1)} %all-to-all-done.refs_0_) | copy-start | bytes 3538948
  55.3 24.2 %copy-start.2 = (bf16[8,2,3,64,128]{4,3,2,1,0:T(8,128)(2,1)}, bf16[8,2,3,64,128]{4,3,2,1,0:T(8,128)(2,1)S(1)}, u32[]{:S(2)}) copy-start(bf16[8,2,3,64,128]{4,3,2,1,0:T(8,128)(2,1)S(1)} %slice.4.refs_1_) | copy-start | bytes 2359300
  55.3 19.5 %collective-permute-start.11 = (bf16[8,2,3,64,128]{4,3,2,1,0:T(8,128)(2,1)S(1)}, bf16[8,2,3,64,128]{4,3,2,1,0:T(8,128)(2,1)S(1)}, u32[]{:S(2)}, u32[]{:S(2)}) collective-permute-start(bf16[8,2,3,64,128]{4,3,2,1,0:T(8,128)(2,1)S(1)} %slice.4.refs_1_), channel_id=1, source_target_pairs={{0,16},{16,0},{1,17},{17,1},{2,18},{18,2},{3,19},{19,3},{4,20},{20... | collective-permute-start | bytes 2359304 | tf_op jit(solution)/shard_map/ppermute | solution.py:218
  56.0 19.8 %collective-permute-start.4 = (bf16[4,3,2,128,128]{4,3,2,1,0:T(8,128)(2,1)S(1)}, bf16[4,3,2,128,128]{4,3,2,1,0:T(8,128)(2,1)S(1)}, u32[]{:S(2)}, u32[]{:S(2)}) collective-permute-start(bf16[4,3,2,128,128]{4,3,2,1,0:T(8,128)(2,1)S(1)} %pad_maximum_fusion.refs_1_), channel_id=1, source_target_pairs={{0,192},{64,0},{128,64},{192,128},{1,193},{65,1},{129,65},{193,129... | collective-permute-start | bytes 2359304 | tf_op jit(solution)/shard_map/ppermute | solution.py:218
  59.0 20.1 %collective-permute-start.3 = (bf16[4,3,2,128,128]{4,3,2,1,0:T(8,128)(2,1)S(1)}, bf16[4,3,2,128,128]{4,3,2,1,0:T(8,128)(2,1)S(1)}, u32[]{:S(2)}, u32[]{:S(2)}) collective-permute-start(bf16[4,3,2,128,128]{4,3,2,1,0:T(8,128)(2,1)S(1)} %pad_maximum_fusion.refs_1_), channel_id=1, source_target_pairs={{0,64},{64,128},{128,192},{192,0},{1,65},{65,129},{129,193},{193,1... | collective-permute-start | bytes 2359304 | tf_op jit(solution)/shard_map/ppermute | solution.py:218
  59.0 20.1 %collective-permute-start.10 = (bf16[8,2,3,64,128]{4,3,2,1,0:T(8,128)(2,1)S(1)}, bf16[8,2,3,64,128]{4,3,2,1,0:T(8,128)(2,1)S(1)}, u32[]{:S(2)}, u32[]{:S(2)}) collective-permute-start(bf16[8,2,3,64,128]{4,3,2,1,0:T(8,128)(2,1)S(1)} %slice.4.refs_1_), channel_id=1, source_target_pairs={{0,1},{1,0},{2,3},{3,2},{4,5},{5,4},{6,7},{7,6},{8,9},{9,8},{10,11... | collective-permute-start | bytes 2359304 | tf_op jit(solution)/shard_map/ppermute | solution.py:218
  59.0 43.1 %copy-start.3 = (bf16[4,3,2,128,128]{4,3,2,1,0:T(8,128)(2,1)}, bf16[4,3,2,128,128]{4,3,2,1,0:T(8,128)(2,1)S(1)}, u32[]{:S(2)}) copy-start(bf16[4,3,2,128,128]{4,3,2,1,0:T(8,128)(2,1)S(1)} %collective-permute-done.5.refs_4_) | copy-start | bytes 2359300
  59.0 43.1 %collective-permute-start.6 = (bf16[4,3,2,128,128]{4,3,2,1,0:T(8,128)(2,1)S(1)}, bf16[4,3,2,128,128]{4,3,2,1,0:T(8,128)(2,1)S(1)}, u32[]{:S(2)}, u32[]{:S(2)}) collective-permute-start(bf16[4,3,2,128,128]{4,3,2,1,0:T(8,128)(2,1)S(1)} %pad_maximum_fusion.refs_1_), channel_id=1, source_target_pairs={{0,1},{1,0},{2,3},{3,2},{4,5},{5,4},{6,7},{7,6},{8,9},{9,8},{10,11... | collective-permute-start | bytes 2359304 | tf_op jit(solution)/shard_map/ppermute | solution.py:218
  74.8 4.7 %copy-start.7 = (bf16[8,2,3,64,128]{4,3,2,1,0:T(8,128)(2,1)}, bf16[8,2,3,64,128]{4,3,2,1,0:T(8,128)(2,1)S(1)}, u32[]{:S(2)}) copy-start(bf16[8,2,3,64,128]{4,3,2,1,0:T(8,128)(2,1)S(1)} %collective-permute-done.11.refs_3_) | copy-start | bytes 2359300
  74.8 4.7 %collective-permute-start.12 = (bf16[8,2,3,64,128]{4,3,2,1,0:T(8,128)(2,1)S(1)}, bf16[8,2,3,64,128]{4,3,2,1,0:T(8,128)(2,1)}, u32[]{:S(2)}, u32[]{:S(2)}) collective-permute-start(bf16[8,2,3,64,128]{4,3,2,1,0:T(8,128)(2,1)S(1)} %collective-permute-done.11.refs_3_), channel_id=1, source_target_pairs={{0,1},{1,0},{2,3},{3,2},{4,5},{5,4},{6,7},{7,6},{8,9},{9,8},{10,11... | collective-permute-start | bytes 2359304 | tf_op jit(solution)/shard_map/ppermute | solution.py:218
  75.8 26.2 %copy-start.4 = (bf16[4,3,2,128,128]{4,3,2,1,0:T(8,128)(2,1)}, bf16[4,3,2,128,128]{4,3,2,1,0:T(8,128)(2,1)S(1)}, u32[]{:S(2)}) copy-start(bf16[4,3,2,128,128]{4,3,2,1,0:T(8,128)(2,1)S(1)} %collective-permute-done.4.refs_3_) | copy-start | bytes 2359300
  75.8 26.3 %collective-permute-start.9 = (bf16[4,3,2,128,128]{4,3,2,1,0:T(8,128)(2,1)S(1)}, bf16[4,3,2,128,128]{4,3,2,1,0:T(8,128)(2,1)S(1)}, u32[]{:S(2)}, u32[]{:S(2)}) collective-permute-start(bf16[4,3,2,128,128]{4,3,2,1,0:T(8,128)(2,1)S(1)} %collective-permute-done.5.refs_4_), channel_id=1, source_target_pairs={{0,1},{1,0},{2,3},{3,2},{4,5},{5,4},{6,7},{7,6},{8,9},{9,8},{10,11... | collective-permute-start | bytes 2359304 | tf_op jit(solution)/shard_map/ppermute | solution.py:218
  79.0 23.0 %copy-start.5 = (bf16[4,3,2,128,128]{4,3,2,1,0:T(8,128)(2,1)}, bf16[4,3,2,128,128]{4,3,2,1,0:T(8,128)(2,1)S(1)}, u32[]{:S(2)}) copy-start(bf16[4,3,2,128,128]{4,3,2,1,0:T(8,128)(2,1)S(1)} %collective-permute-done.3.refs_2_) | copy-start | bytes 2359300
  79.0 23.1 %collective-permute-start.8 = (bf16[4,3,2,128,128]{4,3,2,1,0:T(8,128)(2,1)S(1)}, bf16[4,3,2,128,128]{4,3,2,1,0:T(8,128)(2,1)}, u32[]{:S(2)}, u32[]{:S(2)}) collective-permute-start(bf16[4,3,2,128,128]{4,3,2,1,0:T(8,128)(2,1)S(1)} %collective-permute-done.4.refs_3_), channel_id=1, source_target_pairs={{0,1},{1,0},{2,3},{3,2},{4,5},{5,4},{6,7},{7,6},{8,9},{9,8},{10,11... | collective-permute-start | bytes 2359304 | tf_op jit(solution)/shard_map/ppermute | solution.py:218
  79.0 0.9 copy-start.8
  79.0 23.1 %collective-permute-start.7 = (bf16[4,3,2,128,128]{4,3,2,1,0:T(8,128)(2,1)S(1)}, bf16[4,3,2,128,128]{4,3,2,1,0:T(8,128)(2,1)}, u32[]{:S(2)}, u32[]{:S(2)}) collective-permute-start(bf16[4,3,2,128,128]{4,3,2,1,0:T(8,128)(2,1)S(1)} %collective-permute-done.3.refs_2_), channel_id=1, source_target_pairs={{0,1},{1,0},{2,3},{3,2},{4,5},{5,4},{6,7},{7,6},{8,9},{9,8},{10,11... | collective-permute-start | bytes 2359304 | tf_op jit(solution)/shard_map/ppermute | solution.py:218
  102.1 0.9 copy-start.6
  102.1 1.2 copy-start.9
